TPU v7x, 32 devices: a whole 2x2x4 slice. The times are simulated.
32 devices in a mesh: rows: 16 (over z, y, x), hid: 2 (over core).
Axes of the slice: x: 2, y: 2, z: 4, core: 2. Of those that a mesh axis runs over, the one named last changes fastest.
Arguments:
- hidden_in: bfloat16 [16, 1024, 768], P('rows', None, 'hid'), may hold values from -6 to 6
- teacher_in: bfloat16 [16, 1024, 768], P('rows', None, 'hid'), may hold values from -6 to 6
- segment_ids: int32 [16, 1024], P('rows'), may hold values from 0 to 7, as said below
- pad_mask: int32 [16, 1024], P('rows'), may hold values from 0 to 1, as said below
- qkv_weight: float32 [3, 768, 768], P(None, None, 'hid'), may hold values from -0.21875 to 0.21875
- qkv_moment1: float32 [3, 768, 768], P(None, None, 'hid'), may hold values from -2.3841858e-07 to 2.3841858e-07
- qkv_moment2: float32 [3, 768, 768], P(None, None, 'hid'), may hold values from 7.055068e-17 to 1.1288108e-15
- out_weight: float32 [768, 768], P('hid'), may hold values from -1.75 to 1.75
- out_moment1: float32 [768, 768], P('hid'), may hold values from -2.3841858e-07 to 2.3841858e-07
- out_moment2: float32 [768, 768], P('hid'), may hold values from 7.055068e-17 to 1.1288108e-15
- up_weight: float32 [768, 3072], P(None, 'hid'), may hold values from -0.21875 to 0.21875
- up_moment1: float32 [768, 3072], P(None, 'hid'), may hold values from -2.3841858e-07 to 2.3841858e-07
- up_moment2: float32 [768, 3072], P(None, 'hid'), may hold values from 7.055068e-17 to 1.1288108e-15
- down_weight: float32 [3072, 768], P('hid'), may hold values from -0.109375 to 0.109375
- down_moment1: float32 [3072, 768], P('hid'), may hold values from -2.3841858e-07 to 2.3841858e-07
- down_moment2: float32 [3072, 768], P('hid'), may hold values from 7.055068e-17 to 1.1288108e-15
- bias_vectors: float32 [6, 768], P(None, 'hid'), may hold values from -1.75 to 1.75
- bias_moment1: float32 [6, 768], P(None, 'hid'), may hold values from -9.536743e-07 to 9.536743e-07
- bias_moment2: float32 [6, 768], P(None, 'hid'), may hold values from 1.1288108e-15 to 1.8060974e-14
- up_bias: float32 [3072], P('hid'), may hold values from -1.75 to 1.75
- up_bias_moment1: float32 [3072], P('hid'), may hold values from -4.7683716e-07 to 4.7683716e-07
- up_bias_moment2: float32 [3072], P('hid'), may hold values from 1.4110136e-16 to 2.2576217e-15
- norm_gains: float32 [2, 768], P(None, 'hid'), may hold values from 0.5 to 1.5
- gain_moment1: float32 [2, 768], P(None, 'hid'), may hold values from -9.536743e-07 to 9.536743e-07
- gain_moment2: float32 [2, 768], P(None, 'hid'), may hold values from 1.1288108e-15 to 1.8060974e-14
- head_gates: float32 [12], P('hid'), may hold values from 0.2 to 1
- layer_gates: float32 [2], replicated, may hold values from 0.5 to 1
- dim_gates: float32 [768], P('hid'), may hold values from 0.2 to 1
- unit_gates: float32 [3072], P('hid'), may hold values from 0.2 to 1
- teacher_qkv: bfloat16 [3, 768, 768], P(None, None, 'hid'), may hold values from -0.21875 to 0.21875
- teacher_out: bfloat16 [768, 768], P('hid'), may hold values from -1.75 to 1.75
- teacher_up: bfloat16 [768, 3072], P(None, 'hid'), may hold values from -0.21875 to 0.21875
- teacher_down: bfloat16 [3072, 768], P('hid'), may hold values from -0.109375 to 0.109375
- teacher_biases: bfloat16 [6, 768], P(None, 'hid'), may hold values from -1.75 to 1.75
- teacher_up_bias: bfloat16 [3072], P('hid'), may hold values from -1.75 to 1.75
- teacher_gains: bfloat16 [2, 768], P(None, 'hid'), may hold values from 0.5 to 1.5
Outputs:
- block_out: bfloat16 [16, 1024, 768], P('rows', None, 'hid')
- input_grad: float32 [16, 1024, 768], P('rows', None, 'hid')
- grad_norm: float32 [], replicated
- qkv_grad: float32 [3, 768, 768], P(None, None, 'hid')
- qkv_new: float32 [3, 768, 768], P(None, None, 'hid')
- qkv_moment2_new: float32 [3, 768, 768], P(None, None, 'hid')
- out_grad: float32 [768, 768], P('hid')
- out_new: float32 [768, 768], P('hid')
- out_moment2_new: float32 [768, 768], P('hid')
- up_grad: float32 [768, 3072], P(None, 'hid')
- up_new: float32 [768, 3072], P(None, 'hid')
- up_moment2_new: float32 [768, 3072], P(None, 'hid')
- down_grad: float32 [3072, 768], P('hid')
- down_new: float32 [3072, 768], P('hid')
- down_moment2_new: float32 [3072, 768], P('hid')
- bias_grad: float32 [6, 768], P(None, 'hid')
- bias_new: float32 [6, 768], P(None, 'hid')
- bias_moment2_new: float32 [6, 768], P(None, 'hid')
- up_bias_grad: float32 [3072], P('hid')
- up_bias_new: float32 [3072], P('hid')
- up_bias_moment2_new: float32 [3072], P('hid')
- gain_grad: float32 [2, 768], P(None, 'hid')
- gain_new: float32 [2, 768], P(None, 'hid')
- gain_moment2_new: float32 [2, 768], P(None, 'hid')
- qkv_copy: bfloat16 [3, 768, 768], P(None, None, 'hid')
- out_copy: bfloat16 [768, 768], P('hid')
- up_copy: bfloat16 [768, 3072], P(None, 'hid')
- down_copy: bfloat16 [3072, 768], P('hid')
Inputs may be any that keep to these rules, and one draw needn't show every extreme that they name: `segment_ids`: along each row the ids start at 0, never fall and rise by at most one from a position to the next, so a row holds at most 8 documents; positions with pad_mask 0 keep the id of the row's last real token. `pad_mask`: each row is 1 on a prefix of 307 positions or more and 0 after it.
All inputs are finite; a program needn't handle non-finite values.
Results may differ from a plain program's by a relative error of at most 0.012.
Values may be sent and summed in bfloat16 or wider, within the bound.
A program may use at most 256 MiB of HBM per device.

v0:
```python
import jax
import jax.numpy as jnp
from jax import lax
from jax.sharding import PartitionSpec as P

D = 768
HEAD = 64
STEP = 10


epsilon_norm = 1e-06
masked_score = -1000000000.0
clip_norm = 0.001
beta_first = 0.9
beta_second = 0.999
adam_epsilon = 1e-08
weight_decay = 0.01
rate_attend = 0.03
rate_output = 0.2
rate_expand = 0.03
rate_reduce = 0.03
rate_vector = 0.3


def features(value):
    return lax.all_gather(value, "hid", axis=1, tiled=True)


def spread_sum(partial_rows):
    return lax.psum_scatter(partial_rows, "hid", scatter_dimension=1, tiled=True)


def grad_gather(value):
    return lax.all_gather(value, "hid", axis=1, tiled=True)


def grad_spread(partial_rows):
    return lax.psum_scatter(
        partial_rows.astype(jnp.bfloat16), "hid", scatter_dimension=1, tiled=True
    ).astype(jnp.float32)


def gelu_exact(preact):
    return jax.nn.gelu(preact, approximate=False)


def layer_norm(resid, gain, shift):
    totals, squares = lax.psum((jnp.sum(resid, axis=1), jnp.sum(resid * resid, axis=1)), "hid")
    center = totals / D
    inverse = lax.rsqrt(squares / D - center * center + epsilon_norm)
    normed = (resid - center[:, None]) * inverse[:, None]
    return (normed * gain + shift, normed, inverse)


def norm_back(grad_normed, normed, inverse):
    totals, crossed = lax.psum(
        (jnp.sum(grad_normed, axis=1), jnp.sum(grad_normed * normed, axis=1)), "hid"
    )
    return inverse[:, None] * (grad_normed - totals[:, None] / D - normed * crossed[:, None] / D)


def masked_scores(queries, keys_in, segment, padding):
    raw_score = jnp.einsum("qhd,khd->hqk", queries, keys_in, preferred_element_type=jnp.float32)
    allowed = (segment[:, None] == segment[None, :]) & (padding[None, :] > 0)
    return jnp.where(allowed[None], raw_score * HEAD ** (-0.5), masked_score)


def attend_block(inputs):
    queries, keys_in, values, segment, padding = inputs
    scores = masked_scores(queries, keys_in, segment, padding)
    top_score = jnp.max(scores, axis=-1, keepdims=True)
    weights = jnp.exp(scores - top_score)
    totals = jnp.sum(weights, axis=-1, keepdims=True)
    probs = (weights / totals).astype(jnp.bfloat16)
    context = jnp.einsum("hqk,khd->qhd", probs, values, preferred_element_type=jnp.float32)
    return (context, (top_score + jnp.log(totals))[..., 0])


def attend_back(inputs):
    queries, keys_in, values, segment, padding, log_total, grad_context = inputs
    scores = masked_scores(queries, keys_in, segment, padding)
    probs = jnp.exp(scores - log_total[..., None])
    grad_probs = jnp.einsum(
        "qhd,khd->hqk", grad_context, values, preferred_element_type=jnp.float32
    )
    inner_sum = jnp.sum(probs * grad_probs, axis=-1, keepdims=True)
    grad_raw = (probs * (grad_probs - inner_sum) * HEAD ** (-0.5)).astype(jnp.bfloat16)
    grad_query = jnp.einsum("hqk,khd->qhd", grad_raw, keys_in, preferred_element_type=jnp.float32)
    grad_key = jnp.einsum("hqk,qhd->khd", grad_raw, queries, preferred_element_type=jnp.float32)
    grad_value = jnp.einsum(
        "hqk,qhd->khd", probs.astype(jnp.bfloat16), grad_context, preferred_element_type=jnp.float32
    )
    return (grad_query, grad_key, grad_value)


def forward(hidden, weights, gates, segment_ids, pad_mask):
    qkv_low, out_low, up_low, down_low, biases, up_bias, gains = weights
    head_gates, layer_gates, dim_gates, unit_gates = gates
    seqs_here, length = segment_ids.shape
    width_here = hidden.shape[2]
    tokens_here = seqs_here * length
    heads_here = head_gates.shape[0]
    head_size = width_here // heads_here
    head_shape = (seqs_here, length, heads_here, head_size)
    flat_low = hidden.reshape(tokens_here, width_here)
    gathered = features(flat_low)
    zero_bias = jnp.zeros_like(biases[0])
    projected = jnp.einsum("td,jdc->tjc", gathered, qkv_low, preferred_element_type=jnp.float32)
    projected = (projected + jnp.stack([biases[0], zero_bias, biases[1]])[None]).astype(
        jnp.bfloat16
    )
    queries = projected[:, 0].reshape(head_shape)
    keys_in = projected[:, 1].reshape(head_shape)
    values = projected[:, 2].reshape(head_shape)
    context, log_total = lax.map(attend_block, (queries, keys_in, values, segment_ids, pad_mask))
    gated = context.reshape(tokens_here, heads_here, head_size) * head_gates[None, :, None]
    context_low = gated.reshape(tokens_here, width_here).astype(jnp.bfloat16)
    attended = spread_sum(jnp.dot(context_low, out_low, preferred_element_type=jnp.float32))
    resid_one = flat_low.astype(jnp.float32) + layer_gates[0] * (attended + biases[2]) * dim_gates
    first_out, normed_one, inverse_one = layer_norm(resid_one, gains[0], biases[4])
    first_all = features(first_out.astype(jnp.bfloat16))
    expanded = jnp.dot(first_all, up_low, preferred_element_type=jnp.float32) + up_bias
    activated = (gelu_exact(expanded) * unit_gates).astype(jnp.bfloat16)
    reduced = spread_sum(jnp.dot(activated, down_low, preferred_element_type=jnp.float32))
    resid_two = first_out + layer_gates[1] * (reduced + biases[3]) * dim_gates
    second_out, normed_two, inverse_two = layer_norm(resid_two, gains[1], biases[5])
    kept = (
        gathered,
        queries,
        keys_in,
        values,
        log_total,
        context_low,
        normed_one,
        inverse_one,
        first_all,
        expanded,
        activated,
        normed_two,
        inverse_two,
    )
    return (first_out, second_out, kept)


def adam_step(weight, first, second, grad, rate, decay):
    first_new = beta_first * first + (1.0 - beta_first) * grad
    second_new = beta_second * second + (1.0 - beta_second) * grad * grad
    first_hat = first_new / (1.0 - beta_first**STEP)
    second_hat = second_new / (1.0 - beta_second**STEP)
    return (
        weight - rate * (first_hat / (jnp.sqrt(second_hat) + adam_epsilon) + decay * weight),
        second_new,
    )


def on_device(
    hidden_in,
    teacher_in,
    segment_ids,
    pad_mask,
    qkv_weight,
    qkv_moment1,
    qkv_moment2,
    out_weight,
    out_moment1,
    out_moment2,
    up_weight,
    up_moment1,
    up_moment2,
    down_weight,
    down_moment1,
    down_moment2,
    bias_vectors,
    bias_moment1,
    bias_moment2,
    up_bias,
    up_bias_moment1,
    up_bias_moment2,
    norm_gains,
    gain_moment1,
    gain_moment2,
    head_gates,
    layer_gates,
    dim_gates,
    unit_gates,
    teacher_qkv,
    teacher_out,
    teacher_up,
    teacher_down,
    teacher_biases,
    teacher_up_bias,
    teacher_gains,
):
    seqs_here, length = segment_ids.shape
    width_here = hidden_in.shape[2]
    tokens_here = seqs_here * length
    heads_here = head_gates.shape[0]
    head_size = width_here // heads_here
    head_shape = (seqs_here, length, heads_here, head_size)
    teacher_weights = (
        teacher_qkv,
        teacher_out,
        teacher_up,
        teacher_down,
        teacher_biases.astype(jnp.float32),
        teacher_up_bias.astype(jnp.float32),
        teacher_gains.astype(jnp.float32),
    )
    unit_ones = (
        jnp.ones_like(head_gates),
        jnp.ones_like(layer_gates),
        jnp.ones_like(dim_gates),
        jnp.ones_like(unit_gates),
    )
    teacher_first, teacher_second, teacher_kept = forward(
        teacher_in, teacher_weights, unit_ones, segment_ids, pad_mask
    )
    qkv_low = qkv_weight.astype(jnp.bfloat16)
    out_low = out_weight.astype(jnp.bfloat16)
    up_low = up_weight.astype(jnp.bfloat16)
    down_low = down_weight.astype(jnp.bfloat16)
    student_weights = (qkv_low, out_low, up_low, down_low, bias_vectors, up_bias, norm_gains)
    student_gates = (head_gates, layer_gates, dim_gates, unit_gates)
    first_out, second_out, kept = forward(
        hidden_in, student_weights, student_gates, segment_ids, pad_mask
    )
    (
        gathered,
        queries,
        keys_in,
        values,
        log_total,
        context_low,
        normed_one,
        inverse_one,
        first_all,
        expanded,
        activated,
        normed_two,
        inverse_two,
    ) = kept
    valid = pad_mask.reshape(-1).astype(jnp.float32)
    total_valid = lax.psum(jnp.sum(valid), "rows")
    scale_rows = 2.0 * valid / (D * total_valid)
    grad_second = scale_rows[:, None] * (second_out - teacher_second)
    grad_first = scale_rows[:, None] * (first_out - teacher_first)
    grad_gain_two = jnp.sum(grad_second * normed_two, axis=0)
    grad_shift_two = jnp.sum(grad_second, axis=0)
    grad_resid_two = norm_back(grad_second * norm_gains[1], normed_two, inverse_two)
    grad_reduced = grad_resid_two * (layer_gates[1] * dim_gates)
    grad_down_bias = jnp.sum(grad_reduced, axis=0)
    grad_reduced_all = grad_gather(grad_reduced.astype(jnp.bfloat16))
    grad_activated = (
        jnp.dot(grad_reduced_all, down_low.T, preferred_element_type=jnp.float32)
        .astype(jnp.bfloat16)
        .astype(jnp.float32)
    )
    grad_down = jnp.dot(activated.T, grad_reduced_all, preferred_element_type=jnp.float32)
    gelu_value, gelu_back = jax.vjp(gelu_exact, expanded)
    grad_expanded = gelu_back(grad_activated * unit_gates)[0].astype(jnp.bfloat16)
    grad_up_bias = jnp.sum(grad_expanded.astype(jnp.float32), axis=0)
    grad_up = jnp.dot(first_all.T, grad_expanded, preferred_element_type=jnp.float32)
    grad_first_ffn = grad_spread(
        jnp.dot(grad_expanded, up_low.T, preferred_element_type=jnp.float32)
    )
    grad_first = (
        grad_first + grad_resid_two + grad_first_ffn.astype(jnp.bfloat16).astype(jnp.float32)
    )
    grad_gain_one = jnp.sum(grad_first * normed_one, axis=0)
    grad_shift_one = jnp.sum(grad_first, axis=0)
    grad_resid_one = norm_back(grad_first * norm_gains[0], normed_one, inverse_one)
    grad_attended = grad_resid_one * (layer_gates[0] * dim_gates)
    grad_out_bias = jnp.sum(grad_attended, axis=0)
    grad_attended_all = grad_gather(grad_attended.astype(jnp.bfloat16))
    grad_context = jnp.dot(grad_attended_all, out_low.T, preferred_element_type=jnp.float32)
    grad_out = jnp.dot(context_low.T, grad_attended_all, preferred_element_type=jnp.float32)
    grad_heads = (
        (grad_context.reshape(tokens_here, heads_here, head_size) * head_gates[None, :, None])
        .astype(jnp.bfloat16)
        .reshape(head_shape)
    )
    grad_query, grad_key, grad_value = lax.map(
        attend_back, (queries, keys_in, values, segment_ids, pad_mask, log_total, grad_heads)
    )
    grad_proj = jnp.stack(
        [
            grad_query.reshape(tokens_here, width_here),
            grad_key.reshape(tokens_here, width_here),
            grad_value.reshape(tokens_here, width_here),
        ],
        axis=1,
    ).astype(jnp.bfloat16)
    grad_qkv = jnp.einsum("td,tjc->jdc", gathered, grad_proj, preferred_element_type=jnp.float32)
    bias_sums = jnp.sum(grad_proj.astype(jnp.float32), axis=0)
    grad_input_part = grad_spread(
        jnp.einsum("tjc,jdc->td", grad_proj, qkv_low, preferred_element_type=jnp.float32)
    )
    input_grad = grad_input_part.astype(jnp.bfloat16).astype(jnp.float32) + grad_resid_one
    grad_biases = jnp.stack(
        [bias_sums[0], bias_sums[2], grad_out_bias, grad_down_bias, grad_shift_one, grad_shift_two]
    )
    grad_gains = jnp.stack([grad_gain_one, grad_gain_two])
    grad_qkv, grad_out, grad_up, grad_down, grad_biases, grad_up_bias, grad_gains = lax.psum(
        (grad_qkv, grad_out, grad_up, grad_down, grad_biases, grad_up_bias, grad_gains), "rows"
    )
    weight_grads = (grad_qkv, grad_out, grad_up, grad_down, grad_biases, grad_up_bias, grad_gains)
    local_square = jnp.zeros((), jnp.float32)
    for tensor in weight_grads:
        local_square = local_square + jnp.sum(tensor * tensor)
    grad_norm = jnp.sqrt(lax.psum(local_square, "hid"))
    factor = clip_norm / jnp.maximum(grad_norm, clip_norm)
    weights = (qkv_weight, out_weight, up_weight, down_weight, bias_vectors, up_bias, norm_gains)
    firsts = (
        qkv_moment1,
        out_moment1,
        up_moment1,
        down_moment1,
        bias_moment1,
        up_bias_moment1,
        gain_moment1,
    )
    seconds = (
        qkv_moment2,
        out_moment2,
        up_moment2,
        down_moment2,
        bias_moment2,
        up_bias_moment2,
        gain_moment2,
    )
    rates = (
        rate_attend,
        rate_output,
        rate_expand,
        rate_reduce,
        rate_vector,
        rate_vector,
        rate_vector,
    )
    decays = (weight_decay, weight_decay, weight_decay, weight_decay, 0.0, 0.0, 0.0)
    results = []
    for index in range(7):
        clipped = weight_grads[index] * factor
        new_weight, new_second = adam_step(
            weights[index], firsts[index], seconds[index], clipped, rates[index], decays[index]
        )
        results.append((clipped, new_weight, new_second))
    block_out = second_out.astype(jnp.bfloat16).reshape(hidden_in.shape)
    input_grad = input_grad.reshape(hidden_in.shape)
    return (
        block_out,
        input_grad,
        grad_norm,
        results[0][0],
        results[0][1],
        results[0][2],
        results[1][0],
        results[1][1],
        results[1][2],
        results[2][0],
        results[2][1],
        results[2][2],
        results[3][0],
        results[3][1],
        results[3][2],
        results[4][0],
        results[4][1],
        results[4][2],
        results[5][0],
        results[5][1],
        results[5][2],
        results[6][0],
        results[6][1],
        results[6][2],
        results[0][1].astype(jnp.bfloat16),
        results[1][1].astype(jnp.bfloat16),
        results[2][1].astype(jnp.bfloat16),
        results[3][1].astype(jnp.bfloat16),
    )


def solution(mesh):
    in_specs = (
        P("rows", None, "hid"),
        P("rows", None, "hid"),
        P("rows", None),
        P("rows", None),
        P(None, None, "hid"),
        P(None, None, "hid"),
        P(None, None, "hid"),
        P("hid", None),
        P("hid", None),
        P("hid", None),
        P(None, "hid"),
        P(None, "hid"),
        P(None, "hid"),
        P("hid", None),
        P("hid", None),
        P("hid", None),
        P(None, "hid"),
        P(None, "hid"),
        P(None, "hid"),
        P("hid"),
        P("hid"),
        P("hid"),
        P(None, "hid"),
        P(None, "hid"),
        P(None, "hid"),
        P("hid"),
        P(),
        P("hid"),
        P("hid"),
        P(None, None, "hid"),
        P("hid", None),
        P(None, "hid"),
        P("hid", None),
        P(None, "hid"),
        P("hid"),
        P(None, "hid"),
    )
    out_specs = (
        P("rows", None, "hid"),
        P("rows", None, "hid"),
        P(),
        P(None, None, "hid"),
        P(None, None, "hid"),
        P(None, None, "hid"),
        P("hid", None),
        P("hid", None),
        P("hid", None),
        P(None, "hid"),
        P(None, "hid"),
        P(None, "hid"),
        P("hid", None),
        P("hid", None),
        P("hid", None),
        P(None, "hid"),
        P(None, "hid"),
        P(None, "hid"),
        P("hid"),
        P("hid"),
        P("hid"),
        P(None, "hid"),
        P(None, "hid"),
        P(None, "hid"),
        P(None, None, "hid"),
        P("hid", None),
        P(None, "hid"),
        P("hid", None),
    )
    return jax.shard_map(
        on_device, mesh=mesh, in_specs=in_specs, out_specs=out_specs, check_vma=False
    )
```

profile of v0, /device:TPU:0, one launch (start us, length us, event | category | flops | bytes accessed | tf_op | source)
XLA Modules:
  0.0 932.9 jit_solution(13402009577858339912)
XLA Ops:
  14.6 7.5 all-gather.17.cloned.1.call-done
  40.1 15.3 %fusion.163 = (f32[6,1024]{1,0:T(8,128)S(1)}, f32[6,1024,1024]{1,2,0:T(8,128)}) fusion(pred[1024,1024]{0,1:T(8,128)(4,1)S(1)} %compare_and_fusion, bf16[1024,6,64]{0,2,1:T(8,128)(2,1)} %bitcast.109, bf16[1024,6,64]{0,2,1:T(8,128)(2,1)} %bitcast.108), kind=kOutput, calls=%fused_computation.258 | convolution fusion | flops 830473216 | bytes 27811840 | tf_op jit(solution)/shard_map/while/body/eval_jaxpr/sub | solution.py:72
  55.4 10.8 %fusion.74 = bf16[6,64,1024]{2,1,0:T(8,128)(2,1)S(1)} fusion(bf16[1024,6,64]{0,2,1:T(8,128)(2,1)} %bitcast.107, f32[6,1024,1024]{1,2,0:T(8,128)} %get-tuple-element.280, f32[6,1024]{1,0:T(8,128)S(1)} %get-tuple-element.279), kind=kOutput, calls=%fused_computation.132 | convolution fusion | flops 818282496 | bytes 26763264 | tf_op jit(solution)/shard_map/while/body/eval_jaxpr/hqk,khd->qhd/dot_general | solution.py:75
  68.9 13.0 %fusion.5 = (f32[6,1024]{1,0:T(8,128)S(1)}, f32[6,1024,1024]{1,2,0:T(8,128)}) fusion(pred[1024,1024]{0,1:T(8,128)(4,1)S(1)} %compare_and_fusion, bf16[1024,6,64]{0,2,1:T(8,128)(2,1)} %bitcast.101, bf16[1024,6,64]{0,2,1:T(8,128)(2,1)} %bitcast.103), kind=kOutput, calls=%fused_computation.14 | convolution fusion | flops 824174592 | bytes 27811840 | tf_op jit(solution)/shard_map/while/body/eval_jaxpr/qhd,khd->hqk/dot_general | solution.py:63
  81.9 11.3 %fusion.3 = f32[6,1024]{1,0:T(8,128)S(1)} fusion(f32[6,1024,1024]{1,2,0:T(8,128)} %get-tuple-element.278, f32[6,1024]{1,0:T(8,128)S(1)} %get-tuple-element.277, pred[1024,1024]{0,1:T(8,128)(4,1)S(1)} %compare_and_fusion), kind=kLoop, calls=%fused_computation.12 | loop fusion | flops 25159680 | bytes 26263552 | tf_op jit(solution)/shard_map/while/body/eval_jaxpr/reduce_sum | solution.py:73
  93.3 11.8 %fusion.38 = f32[6,64,1024]{2,1,0:T(8,128)S(1)} fusion(bf16[1024,6,64]{0,2,1:T(8,128)(2,1)S(1)} %bitcast.105, f32[6,1024,1024]{1,2,0:T(8,128)} %get-tuple-element.278, f32[6,1024]{1,0:T(8,128)S(1)} %fusion.3, f32[6,1024]{1,0:T(8,128)S(1)} %get-tuple-element.277, pred[1024,1024]{0,1:T(8,128)(4,1)S(1)} %compare_and_fusion), kind=kOutput, calls=%fused_computation.32 | convolution fusion | flops 836763648 | bytes 28622848 | tf_op jit(solution)/shard_map/while/body/eval_jaxpr/hqk,khd->qhd/dot_general | solution.py:75
  112.6 8.5 reduce-scatter.11.cloned.1.call-done
  141.1 21.2 %fusion.60 = f32[1024,768]{1,0:T(8,128)} fusion(bf16[1536,768]{1,0:T(8,128)(2,1)S(1)} %copy-done, bf16[1024,768]{1,0:T(8,128)(2,1)} %all-gather.11.cloned.1.call-done, bf16[768,1536]{1,0:T(8,128)(2,1)} %param.67, f32[1536]{0:T(1024)S(1)} %convert_element_type.158), kind=kOutput, calls=%fused_computation.92 | convolution fusion | flops 4935647232 | bytes 9443328 | tf_op jit(solution)/shard_map/dot_general | solution.py:124
  162.4 20.1 %multiply_convert_fusion.1 = (bf16[1024,1536]{1,0:T(8,128)(2,1)S(1)}, f32[1024,1536]{1,0:T(8,128)}, f32[1024,1536]{1,0:T(8,128)}) fusion(f32[1536]{0:T(1024)S(1)} %copy-done.49, f32[1536]{0:T(1024)S(1)} %copy-done.40, bf16[1024,768]{1,0:T(8,128)(2,1)} %all-gather.9.cloned.1.call-done, f32[768,1536]{1,0:T(8,128)} %param.46), kind=kOutput, calls=%fused_computation.56 | convolution fusion | flops 2522480640 | bytes 22032384 | tf_op jit(solution)/shard_map/dot_general | solution.py:122
  184.2 6.8 fusion.79
  191.6 42.8 %psum.151 = f32[]{:T(128)} all-reduce(f32[]{:T(128)} %convert_reduce_fusion.2), channel_id=1, replica_groups=mesh['rows'=16,'hid'=2] {'rows'}, use_global_device_ids=true, to_apply=%region_13.14 | all-reduce | flops 1 | bytes 8 | tf_op jit(solution)/shard_map/psum | solution.py:243
  263.6 11.2 %convert_reduce_fusion = (f32[1536]{0:T(1024)S(1)}, bf16[1024,1536]{1,0:T(8,128)(2,1)S(1)}) fusion(f32[1024,1536]{1,0:T(8,128)} %get-tuple-element.242, f32[1536]{0:T(1024)S(1)} %copy-done.50, bf16[1024,768]{1,0:T(8,128)(2,1)} %all-gather.13.cloned.1.call-done, f32[1536,768]{1,0:T(8,128)} %param.49, f32[1024,1536]{1,0:T(8,128)} %get-tuple-element.281, ...), kind=kOutput, calls=%fused_computation.41 | convolution fusion | flops 2448554496 | bytes 22038528 | tf_op jit(solution)/shard_map/dot_general | solution.py:254
  285.2 10.3 %reduce-scatter.19.cloned.1.call-done = bf16[384,1024]{1,0:T(8,128)(2,1)} async-done(((bf16[768,1024]{1,0:T(8,128)(2,1)}), bf16[384,1024]{1,0:T(8,128)(2,1)}) %reduce-scatter.19.cloned.1.call-update) | async-done | bytes 786448
  307.2 10.6 %all-gather.15.cloned.1.call-done = bf16[1024,768]{1,0:T(8,128)(2,1)} async-done(((bf16[1024,384]{1,0:T(8,128)(2,1)}), bf16[1024,768]{1,0:T(8,128)(2,1)}) %all-gather.15.cloned.1.call-update) | async-done | bytes 1572880 | tf_op jit(solution)/shard_map/all_gather | solution.py:34
  321.5 10.0 %fusion.142 = f32[6,1024,1024]{1,2,0:T(8,128)} fusion(bf16[1024,6,64]{0,2,1:T(8,128)(2,1)S(1)} %bitcast.106, f32[1024,6,64]{0,2,1:T(8,128)S(1)} %bitcast.97, f32[6]{0:T(128)S(1)} %copy-done.33), kind=kOutput, calls=%fused_computation.244 | convolution fusion | flops 806092800 | bytes 27525144 | tf_op jit(solution)/shard_map/while/body/eval_jaxpr/qhd,khd->hqk/dot_general | solution.py:83
  331.5 35.2 %fusion.68 = bf16[6,64,1024]{2,1,0:T(8,128)(2,1)} fusion(bf16[1024,6,64]{0,2,1:T(8,128)(2,1)} %bitcast.104, f32[6,1024,1024]{1,2,0:T(8,128)} %fusion.142, f32[6,1024,1024]{1,2,0:T(8,128)} %get-tuple-element.278, f32[6,1024]{1,0:T(8,128)S(1)} %log_add_fusion, pred[1024,1024]{0,1:T(8,128)(4,1)S(1)} %compare_and_fusion), kind=kOutput, calls=%fused_computation.130 | convolution fusion | flops 874912768 | bytes 52977664 | tf_op jit(solution)/shard_map/while/body/eval_jaxpr/hqk,khd->qhd/dot_general | solution.py:88
  366.7 35.3 %fusion.71 = bf16[6,64,1024]{2,1,0:T(8,128)(2,1)} fusion(bf16[1024,6,64]{0,2,1:T(8,128)(2,1)S(1)} %bitcast.102, f32[6,1024,1024]{1,2,0:T(8,128)} %fusion.142, f32[6,1024,1024]{1,2,0:T(8,128)} %get-tuple-element.278, f32[6,1024]{1,0:T(8,128)S(1)} %log_add_fusion, pred[1024,1024]{0,1:T(8,128)(4,1)S(1)} %compare_and_fusion), kind=kOutput, calls=%fused_computation.131 | convolution fusion | flops 874912768 | bytes 52977664 | tf_op jit(solution)/shard_map/while/body/eval_jaxpr/hqk,qhd->khd/dot_general | solution.py:89
  402.1 12.9 %fusion.65 = bf16[6,64,1024]{2,1,0:T(8,128)(2,1)} fusion(f32[6,1024,1024]{1,2,0:T(8,128)} %get-tuple-element.278, f32[6,1024]{1,0:T(8,128)S(1)} %log_add_fusion, pred[1024,1024]{0,1:T(8,128)(4,1)S(1)} %compare_and_fusion, f32[1024,6,64]{0,2,1:T(8,128)} %bitcast.98, f32[6]{0:T(128)S(1)} %copy-done.33), kind=kOutput, calls=%fused_computation.129 | convolution fusion | flops 831651840 | bytes 28598296 | tf_op jit(solution)/shard_map/while/body/eval_jaxpr/hqk,qhd->khd/dot_general | solution.py:90
  427.8 7.4 fusion.167
  463.1 81.5 %all-reduce = (f32[6,384]{1,0:T(8,128)S(1)}, f32[1536]{0:T(1024)S(1)}, f32[2,384]{1,0:T(2,128)S(1)}) all-reduce(f32[6,384]{1,0:T(8,128)S(1)} %stack.41, f32[1536]{0:T(1024)S(1)} %get-tuple-element.282, f32[2,384]{1,0:T(2,128)S(1)} %pad_maximum_fusion.3), channel_id=1, replica_groups=mesh['rows'=16,'hid'=2] {'rows'}, use_global_device_ids=true, to_apply=%region_50.51 | all-reduce | flops 4608 | bytes 36864 | tf_op jit(solution)/shard_map/psum | solution.py:303
  547.9 297.9 %all-reduce.8.cloned.1.call-done = (f32[3,768,384]{1,2,0:T(8,128)}, f32[384,768]{1,0:T(8,128)}, f32[768,1536]{1,0:T(8,128)}, f32[1536,768]{1,0:T(8,128)}) async-done(((f32[3,768,384]{1,2,0:T(8,128)}, f32[384,768]{1,0:T(8,128)}, f32[768,1536]{1,0:T(8,128)}, f32[1536,768]{1,0:T(8,128)}), (f32[3,768,384]{1,2,0:T(8,128)}, f32[384,768]{1,0:T(8,128)}, f32[768,1536]{1,0:T(8,128)}, ...) | async-done | bytes 14155792 | tf_op jit(solution)/shard_map/psum | solution.py:303
  865.5 8.1 fusion.152
  897.5 13.2 %fusion.146 = (bf16[1536,768]{1,0:T(8,128)(2,1)}, f32[1536,768]{1,0:T(8,128)}, f32[1536,768]{1,0:T(8,128)}, f32[1536,768]{1,0:T(8,128)}) fusion(f32[1536,768]{1,0:T(8,128)} %param.49, f32[1536,768]{1,0:T(8,128)} %param.50, f32[1536,768]{1,0:T(8,128)} %param.51, f32[1536,768]{1,0:T(8,128)} %get-tuple-element.196, f32[]{:T(128)S(6)} %div.200), kind=kLoop, calls=%fused_computation.248 | loop fusion | flops 20054016 | bytes 35389444 | tf_op jit(solution)/shard_map/convert_element_type | solution.py:378
  910.8 11.7 %fusion.148 = (bf16[768,1536]{1,0:T(8,128)(2,1)}, f32[768,1536]{1,0:T(8,128)}, f32[768,1536]{1,0:T(8,128)}, f32[768,1536]{1,0:T(8,128)}) fusion(f32[768,1536]{1,0:T(8,128)} %param.46, f32[768,1536]{1,0:T(8,128)} %param.47, f32[768,1536]{1,0:T(8,128)} %param.48, f32[768,1536]{1,0:T(8,128)S(1)} %bitcast.96, f32[]{:T(128)S(6)} %div.200), kind=kLoop, calls=%fused_computation.249 | loop fusion | flops 20054016 | bytes 35389444 | tf_op jit(solution)/shard_map/convert_element_type | solution.py:377
  (234 shorter events, 196.2 us)
Async XLA Ops:
  7.2 133.9 %copy-start = (bf16[1536,768]{1,0:T(8,128)(2,1)S(1)}, bf16[1536,768]{1,0:T(8,128)(2,1)}, u32[]{:S(2)}) copy-start(bf16[1536,768]{1,0:T(8,128)(2,1)} %param.68) | copy-start | bytes 7077892
  7.2 14.9 %all-gather.17.cloned.1.call-start = ((), (), s32[]{:S(2)}) async-start(), calls=%async_computation.14 | async-start | bytes 2359296 | tf_op jit(solution)/shard_map/all_gather | solution.py:26
  8.0 26.6 %all-gather.19.cloned.1.call-start = ((), (), s32[]{:S(2)}) async-start(), calls=%async_computation.15 | async-start | bytes 2359296 | tf_op jit(solution)/shard_map/all_gather | solution.py:26
  8.7 100.9 %reduce-scatter.15.cloned.1.call-start = ((), (), s32[]{:S(2)}) async-start(), calls=%async_computation.9 | async-start | bytes 4718592 | tf_op jit(solution)/shard_map/reduce_scatter | solution.py:30
  68.9 52.2 %reduce-scatter.11.cloned.1.call-start = ((), (), s32[]{:S(2)}) async-start(), calls=%async_computation.6 | async-start | bytes 4718592 | tf_op jit(solution)/shard_map/reduce_scatter | solution.py:30
  108.9 32.2 %all-gather.11.cloned.1.call-start = ((), (), s32[]{:S(2)}) async-start(), calls=%async_computation.10 | async-start | bytes 2359296 | tf_op jit(solution)/shard_map/all_gather | solution.py:26
  109.6 20.3 %copy-start.43 = (bf16[1536]{0:T(1024)(128)(2,1)S(1)}, bf16[1536]{0:T(1024)(128)(2,1)}, u32[]{:S(2)}) copy-start(bf16[1536]{0:T(1024)(128)(2,1)} %param.70) | copy-start | bytes 9220
  109.6 20.3 %copy-start.34 = (f32[2,384]{1,0:T(2,128)S(1)}, f32[2,384]{1,0:T(2,128)}, u32[]{:S(2)}) copy-start(f32[2,384]{1,0:T(2,128)} %param.58) | copy-start | bytes 9220
  129.9 32.5 %all-gather.9.cloned.1.call-start = ((), (), s32[]{:S(2)}) async-start(), calls=%async_computation.7 | async-start | bytes 2359296 | tf_op jit(solution)/shard_map/all_gather | solution.py:26
  134.2 28.2 %copy-start.40 = (f32[1536]{0:T(1024)S(1)}, f32[1536]{0:T(1024)}, u32[]{:S(2)}) copy-start(f32[1536]{0:T(1024)} %param.55) | copy-start | bytes 18436
  134.2 28.2 %copy-start.49 = (f32[1536]{0:T(1024)S(1)}, f32[1536]{0:T(1024)}, u32[]{:S(2)}) copy-start(f32[1536]{0:T(1024)} %param.64) | copy-start | bytes 18436
  134.2 102.2 %reduce-scatter.17.cloned.1.call-start = ((), (), s32[]{:S(2)}) async-start(), calls=%async_computation.11 | async-start | bytes 4718592 | tf_op jit(solution)/shard_map/reduce_scatter | solution.py:30
  162.3 77.1 %reduce-scatter.13.cloned.1.call-start = ((), (), s32[]{:S(2)}) async-start(), calls=%async_computation.8 | async-start | bytes 4718592 | tf_op jit(solution)/shard_map/reduce_scatter | solution.py:30
  184.2 52.2 %copy-start.4 = (f32[1024,384]{1,0:T(8,128)S(1)}, f32[1024,384]{1,0:T(8,128)}, u32[]{:S(2)}) copy-start(f32[1024,384]{1,0:T(8,128)} %get-tuple-element.245) | copy-start | bytes 4718596
  190.9 48.5 %copy-start.38 = (f32[384]{0:T(512)S(1)}, f32[384]{0:T(512)}, u32[]{:S(2)}) copy-start(f32[384]{0:T(512)} %get-tuple-element.257) | copy-start | bytes 4612
  190.9 72.6 %all-gather.13.cloned.1.call-start = ((), (), s32[]{:S(2)}) async-start(), calls=%async_computation.12 | async-start | bytes 2359296 | tf_op jit(solution)/shard_map/all_gather | solution.py:34
  257.5 38.1 %reduce-scatter.19.cloned.1.call-start = ((), (), s32[]{:S(2)}) async-start(), calls=%async_computation.16 | async-start | bytes 2359296
  285.2 32.6 %all-gather.15.cloned.1.call-start = ((), (), s32[]{:S(2)}) async-start(), calls=%async_computation.13 | async-start | bytes 2359296 | tf_op jit(solution)/shard_map/all_gather | solution.py:34
  305.6 15.9 %copy-start.13 = (bf16[1024,1,384]{0,2,1:T(8,128)(2,1)S(1)}, bf16[1024,1,384]{0,2,1:T(8,128)(2,1)}, u32[]{:S(2)}) copy-start(bf16[1024,1,384]{0,2,1:T(8,128)(2,1)} %get-tuple-element.251) | copy-start | bytes 2359300
  305.6 15.9 %copy-start.33 = (f32[6]{0:T(128)S(1)}, f32[6]{0:T(128)}, u32[]{:S(2)}) copy-start(f32[6]{0:T(128)} %param.61) | copy-start | bytes 76
  306.7 239.7 %reduce-scatter.21.cloned.1.call-start = ((), (), s32[]{:S(2)}) async-start(), calls=%async_computation.17 | async-start | bytes 2359296
  331.5 35.2 %copy-start.11 = (bf16[1024,1,384]{0,2,1:T(8,128)(2,1)S(1)}, bf16[1024,1,384]{0,2,1:T(8,128)(2,1)}, u32[]{:S(2)}) copy-start(bf16[1024,1,384]{0,2,1:T(8,128)(2,1)} %get-tuple-element.250) | copy-start | bytes 2359300
  427.7 418.1 %all-reduce.8.cloned.1.call-start = ((), (), s32[]{:S(2)}) async-start(), calls=%async_computation.18 | async-start | bytes 28311552 | tf_op jit(solution)/shard_map/psum | solution.py:303
  893.4 17.3 %slice-start = ((s8[4718592]{0:T(1024)(128)(4,1)}), s8[524288]{0:T(1024)(128)(4,1)S(1)}, s32[]{:S(2)}) async-start(s8[4718592]{0:T(1024)(128)(4,1)} %bitcast.95), calls=%async_computation.19 | async-start | bytes 1048576
  (43 other events, 314.1 us)
Sparse Core Ops, SparseCore 0:
  9.6 12.4 all-gather.16
  23.6 10.9 all-gather.18
  69.0 12.0 reduce-scatter.14
  109.0 12.0 reduce-scatter.10
  130.0 11.0 all-gather.10
  143.0 10.9 all-gather.8
  162.4 12.0 reduce-scatter.16
  191.1 12.0 reduce-scatter.12
  257.6 5.8 all-gather.12
  285.3 10.2 reduce-scatter.18
  306.8 10.9 all-gather.14
  427.8 10.2 reduce-scatter.20
  446.0 399.7 all-reduce.7
where the time goes:
time: 942 us; the launch traced here: 933 us
  waiting for transfers between devices  355 us (38%)
  matrix products  250 us (27%)
  blocking collectives  139 us (15%)
  other arithmetic  104 us (11%)
  local copies, waits for them, and re-layouts  61.5 us (7%)
  between operations  22.1 us (2%)
    psum x1, waiting for transfers between devices, on_device(): lax.psum((grad_qkv, grad_out, grad_up, grad_down, grad_biases, grad_up_bi...  298 us
    psum x1, blocking collectives, on_device(): lax.psum((grad_qkv, grad_out, grad_up, grad_down, grad_biases, grad_up_bi...  81.5 us
    unnamed x119, local copies, waits for them, and re-layouts  50.3 us
    psum x1, blocking collectives, on_device(): total_valid = lax.psum(jnp.sum(valid), 'rows')  42.8 us
    dot_general x1, matrix products, attend_back(): jnp.einsum('hqk,qhd->khd', grad_raw, queries, preferred_element_type=jnp....  35.3 us
    dot_general x1, matrix products, attend_back(): jnp.einsum('hqk,khd->qhd', grad_raw, keys_in, preferred_element_type=jnp....  35.2 us
    dot_general x2, matrix products, forward(): jnp.dot(activated, down_low, preferred_element_type=jnp.float32)  28 us
    dot_general x2, matrix products, attend_block(): jnp.einsum('hqk,khd->qhd', probs, values, preferred_element_type=jnp.floa...  22.5 us
  transfers between devices with their start and end apart: 13, of which 8 were waited for; matrix products, arithmetic and copies ran while one was open for 16% of the time, Pallas kernels for 0%

commit v1 on v0

--- a/solution.py
+++ b/solution.py
@@ -1,6 +1,10 @@
+import functools
+
 import jax
 import jax.numpy as jnp
 from jax import lax
+from jax.experimental import pallas as pl
+from jax.experimental.pallas import tpu as pltpu
 from jax.sharding import PartitionSpec as P
 
 D = 768
@@ -142,6 +146,246 @@
     return (first_out, second_out, kept)
 
 
+INNER = 16
+BATCHES = 3
+SHARD = 96
+
+
+def reduce_kernel(outer, parts_ref, small_ref, sums_ref, small_out_ref, square_ref, *scratch):
+    (
+        recv_one, send_two, recv_two, keep, send_three, recv_three, shard, outer_recv,
+        small_send, small_recv, small_three, small_outer, square_send, square_recv,
+        send_sems, recv_sems, local_sems,
+    ) = scratch
+    place = lax.axis_index("rows")
+    inside = place % INNER
+    base = place - inside
+    x, y, z = inside % 2, (inside // 2) % 2, inside // 4
+    group = place // INNER
+    core = lax.axis_index("hid")
+    to_x = {"rows": place + 1 - 2 * x}
+    to_y = {"rows": place + 2 - 4 * y}
+    to_z = [{"rows": base + inside % 4 + 4 * ((z + d) % 4)} for d in range(4)]
+    to_group = [{"rows": inside + INNER * ((group + d) % outer)} for d in range(outer)]
+    to_core = {"hid": 1 - core}
+    barrier = pltpu.get_barrier_semaphore()
+    peers = [to_x, to_y] + to_z[1:] + to_group[1:] + [to_core]
+    for peer in peers:
+        pl.semaphore_signal(barrier, inc=1, device_id=peer, device_id_type=pl.DeviceIdType.MESH)
+    pl.semaphore_wait(barrier, len(peers))
+
+    counter = [0]
+    pending = []
+
+    def send(source, target, peer):
+        index = counter[0]
+        counter[0] += 1
+        copy = pltpu.make_async_remote_copy(
+            src_ref=source, dst_ref=target, send_sem=send_sems.at[index],
+            recv_sem=recv_sems.at[index], device_id=peer, device_id_type=pl.DeviceIdType.MESH,
+        )
+        copy.start()
+        pending.append(copy)
+        return copy
+
+    wide = jnp.float32
+    first_bit, second_bit = (x, y), (y, x)
+    first_peer, second_peer = (to_x, to_y), (to_y, to_x)
+
+    def rows(start, size):
+        return pl.ds(pl.multiple_of(start, SHARD), size)
+
+    half = [768 * first_bit[lane] for lane in range(2)]
+    quarter = [half[lane] + 384 * second_bit[lane] for lane in range(2)]
+    mine = [quarter[lane] + SHARD * z for lane in range(2)]
+    one, two, three, four, five, six = {}, {}, {}, {}, {}, {}
+
+    def start_one(b):
+        for lane in range(2):
+            one[b, lane] = send(
+                parts_ref.at[b, lane, rows(768 - half[lane], 768)], recv_one.at[b, lane], first_peer[lane]
+            )
+
+    def start_two(b):
+        for lane in range(2):
+            one[b, lane].wait_recv()
+            other = 384 - 384 * second_bit[lane]
+            send_two[b, lane] = (
+                parts_ref[b, lane, rows(half[lane] + other, 384)].astype(wide)
+                + recv_one[b, lane, rows(other, 384)].astype(wide)
+            ).astype(jnp.bfloat16)
+            two[b, lane] = send(send_two.at[b, lane], recv_two.at[b, lane], second_peer[lane])
+        for lane in range(2):
+            keep[b, lane] = parts_ref[b, lane, rows(quarter[lane], 384)].astype(wide) + recv_one[
+                b, lane, rows(384 * second_bit[lane], 384)
+            ].astype(wide)
+
+    def start_three(b):
+        for lane in range(2):
+            two[b, lane].wait_recv()
+            keep[b, lane] = keep[b, lane] + recv_two[b, lane].astype(wide)
+            for d in (2, 1, 3):
+                send_three[b, lane, d - 1] = keep[
+                    b, lane, rows(SHARD * ((z + d) % 4), SHARD)
+                ].astype(jnp.bfloat16)
+                three[b, lane, d] = send(
+                    send_three.at[b, lane, d - 1], recv_three.at[b, lane, d - 1], to_z[d]
+                )
+
+    squares = []
+
+    def start_four(b):
+        for lane in range(2):
+            total = keep[b, lane, rows(SHARD * z, SHARD)]
+            for d in (1, 3, 2):
+                three[b, lane, d].wait_recv()
+                total = total + recv_three[b, lane, d - 1].astype(wide)
+            if outer > 1:
+                shard[b, lane] = total.astype(jnp.bfloat16)
+                copies = [
+                    send(shard.at[b, lane], outer_recv.at[b, lane, d - 1], to_group[d])
+                    for d in range(1, outer)
+                ]
+                for d, copy in enumerate(copies):
+                    copy.wait()
+                    total = total + outer_recv[b, lane, d].astype(wide)
+            squares.append(jnp.sum(total * total, axis=0, keepdims=True))
+            shard[b, lane] = total.astype(jnp.bfloat16)
+            place_here = sums_ref.at[b, lane, rows(mine[lane], SHARD)]
+            local = pltpu.make_async_copy(shard.at[b, lane], place_here, local_sems.at[b, lane])
+            local.start()
+            four[b, lane] = [send(shard.at[b, lane], place_here, to_z[d]) for d in (2, 1, 3)] + [local]
+
+    def start_five(b):
+        for lane in range(2):
+            for copy in four[b, lane][:3]:
+                copy.wait_recv()
+            four[b, lane][3].wait()
+            block = sums_ref.at[b, lane, rows(quarter[lane], 384)]
+            five[b, lane] = send(block, block, second_peer[lane])
+
+    def start_six(b):
+        for lane in range(2):
+            five[b, lane].wait_recv()
+            block = sums_ref.at[b, lane, rows(half[lane], 768)]
+            six[b, lane] = send(block, block, first_peer[lane])
+
+    def finish(b):
+        for lane in range(2):
+            six[b, lane].wait_recv()
+
+    start_one(0)
+    small_one = send(small_ref, small_recv.at[0], to_x)
+    start_one(1)
+    small_one.wait_recv()
+    small_send[0] = small_ref[...] + small_recv[0]
+    small_two = send(small_send.at[0], small_recv.at[1], to_y)
+    start_two(0)
+    start_one(2)
+    small_two.wait_recv()
+    small_send[1] = small_send[0] + small_recv[1]
+    small_three[z] = small_send[1]
+    small_z = [send(small_send.at[1], small_three.at[z], to_z[d]) for d in range(1, 4)]
+    start_two(1)
+    start_three(0)
+    for copy in small_z:
+        copy.wait_recv()
+    small_total = (small_three[0] + small_three[1]) + (small_three[2] + small_three[3])
+    if outer > 1:
+        small_send[2] = small_total
+        small_outer[group] = small_total
+        copies = [send(small_send.at[2], small_outer.at[group], to_group[d]) for d in range(1, outer)]
+        for copy in copies:
+            copy.wait_recv()
+        small_total = small_outer[0]
+        for index in range(1, outer):
+            small_total = small_total + small_outer[index]
+    small_out_ref[...] = small_total
+    start_two(2)
+    start_three(1)
+    start_four(0)
+    start_three(2)
+    start_four(1)
+    start_five(0)
+    start_four(2)
+    total_square = squares[0]
+    for value in squares[1:]:
+        total_square = total_square + value
+    spread = jnp.broadcast_to(jnp.sum(total_square, axis=1, keepdims=True), (8, 128))
+    square_send[0] = spread
+    square_x = send(square_send.at[0], square_recv.at[0], to_x)
+    start_five(1)
+    start_six(0)
+    square_x.wait_recv()
+    square_send[1] = square_send[0] + square_recv[0]
+    square_y = send(square_send.at[1], square_recv.at[1], to_y)
+    start_five(2)
+    square_y.wait_recv()
+    square_send[2] = square_send[1] + square_recv[1]
+    square_recv[4 + z] = square_send[2]
+    square_z = [send(square_send.at[2], square_recv.at[4 + z], to_z[d]) for d in range(1, 4)]
+    start_six(1)
+    for copy in square_z:
+        copy.wait_recv()
+    small_square = jnp.sum(small_total * small_total, axis=(0, 1), keepdims=True)
+    square_send[3] = (
+        (square_recv[4] + square_recv[5]) + (square_recv[6] + square_recv[7])
+    ) + jnp.broadcast_to(small_square, (8, 128))
+    square_core = send(square_send.at[3], square_recv.at[2], to_core)
+    start_six(2)
+    square_core.wait_recv()
+    square_ref[...] = square_send[3] + square_recv[2]
+    for b in range(BATCHES):
+        finish(b)
+    for copy in pending:
+        copy.wait_send()
+
+
+def reduce_rows(outer, parts, small):
+    low = jnp.bfloat16
+    lanes = (BATCHES, 2)
+    copies = 6 * (1 + 1 + 3 + (outer - 1) + 3 + 1 + 1) + 5 + (outer - 1) + 6
+    small_shape = small.shape
+    return pl.pallas_call(
+        functools.partial(reduce_kernel, outer),
+        out_shape=(
+            jax.ShapeDtypeStruct(parts.shape, low),
+            jax.ShapeDtypeStruct(small_shape, jnp.float32),
+            jax.ShapeDtypeStruct((8, 128), jnp.float32),
+        ),
+        in_specs=[pl.BlockSpec(memory_space=pltpu.VMEM)] * 2,
+        out_specs=(
+            pl.BlockSpec(memory_space=pl.ANY),
+            pl.BlockSpec(memory_space=pltpu.VMEM),
+            pl.BlockSpec(memory_space=pltpu.VMEM),
+        ),
+        scratch_shapes=[
+            pltpu.VMEM(lanes + (768, 384), low),
+            pltpu.VMEM(lanes + (384, 384), low),
+            pltpu.VMEM(lanes + (384, 384), low),
+            pltpu.VMEM(lanes + (384, 384), jnp.float32),
+            pltpu.VMEM(lanes + (3, SHARD, 384), low),
+            pltpu.VMEM(lanes + (3, SHARD, 384), low),
+            pltpu.VMEM(lanes + (SHARD, 384), low),
+            pltpu.VMEM(lanes + (max(outer - 1, 1), SHARD, 384), low),
+            pltpu.VMEM((3,) + small_shape, jnp.float32),
+            pltpu.VMEM((2,) + small_shape, jnp.float32),
+            pltpu.VMEM((4,) + small_shape, jnp.float32),
+            pltpu.VMEM((outer,) + small_shape, jnp.float32),
+            pltpu.VMEM((4, 8, 128), jnp.float32),
+            pltpu.VMEM((8, 8, 128), jnp.float32),
+            pltpu.SemaphoreType.DMA((copies,)),
+            pltpu.SemaphoreType.DMA((copies,)),
+            pltpu.SemaphoreType.DMA(lanes),
+        ],
+        compiler_params=pltpu.CompilerParams(
+            collective_id=0, has_side_effects=True, vmem_limit_bytes=56 * 2**20
+        ),
+        cost_estimate=pl.CostEstimate(flops=10**8, bytes_accessed=3 * 10**8, transcendentals=0),
+        name="reduce_rows",
+    )(parts, small)
+
+
 def adam_step(weight, first, second, grad, rate, decay):
     first_new = beta_first * first + (1.0 - beta_first) * grad
     second_new = beta_second * second + (1.0 - beta_second) * grad * grad
@@ -151,6 +395,47 @@
         weight - rate * (first_hat / (jnp.sqrt(second_hat) + adam_epsilon) + decay * weight),
         second_new,
     )
+
+
+def clip_factor(square):
+    return clip_norm / jnp.maximum(jnp.sqrt(square), clip_norm)
+
+
+def adam_kernel(rate, square_ref, sums_ref, weight_ref, first_ref, second_ref, grad_ref, new_ref, second_new_ref, copy_ref):
+    clipped = sums_ref[...].astype(jnp.float32) * clip_factor(square_ref[:1, :1])
+    grad_ref[...] = clipped
+    new_weight, new_second = adam_step(
+        weight_ref[...], first_ref[...], second_ref[...], clipped, rate, weight_decay
+    )
+    new_ref[...] = new_weight
+    second_new_ref[...] = new_second
+    copy_ref[...] = new_weight.astype(jnp.bfloat16)
+
+
+def adam_call(rate, grid, sums_block, sums_map, block, block_map, square, sums, weight, first, second):
+    shape = weight.shape
+    same = pl.BlockSpec(block, block_map)
+    return pl.pallas_call(
+        functools.partial(adam_kernel, rate),
+        grid=grid,
+        out_shape=(
+            jax.ShapeDtypeStruct(shape, jnp.float32),
+            jax.ShapeDtypeStruct(shape, jnp.float32),
+            jax.ShapeDtypeStruct(shape, jnp.float32),
+            jax.ShapeDtypeStruct(shape, jnp.bfloat16),
+        ),
+        in_specs=[
+            pl.BlockSpec((8, 128), lambda *index: (0, 0)),
+            pl.BlockSpec(sums_block, sums_map),
+            same,
+            same,
+            same,
+        ],
+        out_specs=(same, same, same, same),
+        compiler_params=pltpu.CompilerParams(vmem_limit_bytes=48 * 2**20),
+        cost_estimate=pl.CostEstimate(flops=20 * weight.size, bytes_accessed=28 * weight.size, transcendentals=weight.size),
+        name="adam",
+    )(square, sums, weight, first, second)
 
 
 def on_device(
@@ -300,51 +585,64 @@
         [bias_sums[0], bias_sums[2], grad_out_bias, grad_down_bias, grad_shift_one, grad_shift_two]
     )
     grad_gains = jnp.stack([grad_gain_one, grad_gain_two])
-    grad_qkv, grad_out, grad_up, grad_down, grad_biases, grad_up_bias, grad_gains = lax.psum(
-        (grad_qkv, grad_out, grad_up, grad_down, grad_biases, grad_up_bias, grad_gains), "rows"
-    )
-    weight_grads = (grad_qkv, grad_out, grad_up, grad_down, grad_biases, grad_up_bias, grad_gains)
-    local_square = jnp.zeros((), jnp.float32)
-    for tensor in weight_grads:
-        local_square = local_square + jnp.sum(tensor * tensor)
-    grad_norm = jnp.sqrt(lax.psum(local_square, "hid"))
-    factor = clip_norm / jnp.maximum(grad_norm, clip_norm)
-    weights = (qkv_weight, out_weight, up_weight, down_weight, bias_vectors, up_bias, norm_gains)
-    firsts = (
-        qkv_moment1,
-        out_moment1,
-        up_moment1,
-        down_moment1,
-        bias_moment1,
-        up_bias_moment1,
-        gain_moment1,
-    )
-    seconds = (
-        qkv_moment2,
-        out_moment2,
-        up_moment2,
-        down_moment2,
-        bias_moment2,
-        up_bias_moment2,
-        gain_moment2,
-    )
-    rates = (
-        rate_attend,
-        rate_output,
-        rate_expand,
-        rate_reduce,
-        rate_vector,
-        rate_vector,
-        rate_vector,
-    )
-    decays = (weight_decay, weight_decay, weight_decay, weight_decay, 0.0, 0.0, 0.0)
-    results = []
-    for index in range(7):
-        clipped = weight_grads[index] * factor
-        new_weight, new_second = adam_step(
-            weights[index], firsts[index], seconds[index], clipped, rates[index], decays[index]
-        )
-        results.append((clipped, new_weight, new_second))
+    parts = jnp.stack(
+        [
+            jnp.stack([grad_down[:, :384], grad_down[:, 384:]]),
+            jnp.stack(
+                [
+                    jnp.concatenate([grad_up[:, :384], grad_up[:, 384:768]]),
+                    jnp.concatenate([grad_up[:, 768:1152], grad_up[:, 1152:]]),
+                ]
+            ),
+            jnp.stack(
+                [
+                    jnp.concatenate([grad_qkv[0], grad_qkv[1]]),
+                    jnp.concatenate([grad_qkv[2], grad_out[:, :384], grad_out[:, 384:]]),
+                ]
+            ),
+        ]
+    ).astype(jnp.bfloat16)
+    small = jnp.concatenate(
+        [
+            grad_biases.reshape(-1),
+            grad_up_bias,
+            grad_gains.reshape(-1),
+            jnp.zeros((512,), jnp.float32),
+        ]
+    ).reshape(40, 128)
+    rows_all = lax.axis_size("rows")
+    sums, small_sums, square = reduce_rows(rows_all // INNER, parts, small)
+    grad_norm = jnp.sqrt(square[0, 0])
+    factor = clip_factor(square[0, 0])
+    one = pl.squeezed
+    down_results = adam_call(
+        rate_reduce, (4, 2), (one, one, 384, 384), lambda i, j: (0, j, i, 0), (384, 384), lambda i, j: (i, j),
+        square, sums, down_weight, down_moment1, down_moment2,
+    )
+    up_results = adam_call(
+        rate_expand, (2, 4), (one, one, 384, 384), lambda i, j: (1, j // 2, (j % 2) * 2 + i, 0), (384, 384), lambda i, j: (i, j),
+        square, sums, up_weight, up_moment1, up_moment2,
+    )
+    qkv_results = adam_call(
+        rate_attend, (3, 2), (one, one, 384, 384), lambda i, j: (2, i // 2, (i % 2) * 2 + j, 0), (one, 384, 384), lambda i, j: (i, j, 0),
+        square, sums, qkv_weight, qkv_moment1, qkv_moment2,
+    )
+    out_results = adam_call(
+        rate_output, (2,), (one, one, 384, 384), lambda j: (2, 1, 2 + j, 0), (384, 384), lambda j: (0, j),
+        square, sums, out_weight, out_moment1, out_moment2,
+    )
+    flat_small = small_sums.reshape(-1) * factor
+    small_grads = (
+        flat_small[:2304].reshape(6, 384), flat_small[2304:3840], flat_small[3840:4608].reshape(2, 384)
+    )
+    small_states = (
+        (bias_vectors, bias_moment1, bias_moment2),
+        (up_bias, up_bias_moment1, up_bias_moment2),
+        (norm_gains, gain_moment1, gain_moment2),
+    )
+    results = [qkv_results, out_results, up_results, down_results]
+    for (weight, first, second), clipped in zip(small_states, small_grads):
+        results.append((clipped,) + adam_step(weight, first, second, clipped, rate_vector, 0.0))
     block_out = second_out.astype(jnp.bfloat16).reshape(hidden_in.shape)
     input_grad = input_grad.reshape(hidden_in.shape)
     return (
@@ -372,10 +670,10 @@
         results[6][0],
         results[6][1],
         results[6][2],
-        results[0][1].astype(jnp.bfloat16),
-        results[1][1].astype(jnp.bfloat16),
-        results[2][1].astype(jnp.bfloat16),
-        results[3][1].astype(jnp.bfloat16),
+        results[0][3],
+        results[1][3],
+        results[2][3],
+        results[3][3],
     )
 
 

time: 942 us -> 703 us (0.75)
  waiting for transfers between devices: 355 us -> 33.4 us
  Pallas kernels: 0 us -> 216 us
  blocking collectives: 139 us -> 55.7 us
  other arithmetic: 104 us -> 74.9 us
  local copies, waits for them, and re-layouts: 61.5 us -> 48.4 us
    psum x1 -> x0, waiting for transfers between devices: 298 us -> none  [on_device(): lax.psum((grad_qkv, grad_out, grad_up, grad_down, grad_biases, grad_up_bi...]
    pallas_call x0 -> x5, Pallas kernels: none -> 216 us  [the longest x1 172 us: reduce_rows(): pl.pallas_call(functools.partial(reduce_kernel, outer), out_shape=(jax.Sh...]
    psum x2 -> x0, blocking collectives: 84.4 us -> none  [the longest x1 81.5 us: on_device(): lax.psum((grad_qkv, grad_out, grad_up, grad_down, grad_biases, grad_up_bi...]
    convert_element_type x4 -> x0, other arithmetic: 35.3 us -> none  [the longest x1 13.2 us: on_device(): results[3][1].astype(jnp.bfloat16)]
    unnamed x119 -> x164, local copies, waits for them, and re-layouts: 50.3 us -> 24 us
    reduce_sum x7 -> x0, other arithmetic: 12 us -> none  [on_device(): local_square = local_square + jnp.sum(tensor * tensor)]
    unnamed x15 -> x14, waiting for transfers between devices: 11.9 us -> 1.54 us
    another operation x0 -> x8, other arithmetic: none -> 10.2 us  [the longest x4 7.3 us: on_device(): jnp.stack([jnp.stack([grad_down[:, :384], grad_down[:, 384:]]), jnp.stack...]
  transfers between devices with their start and end apart: 13 -> 12, of which waited for: 8 -> 6; matrix products, arithmetic and copies ran while one was open for 16% -> 22% of each run, Pallas kernels for 0% -> 31%
where the time goes in v1:
time: 703 us; the launch traced here: 693 us
  matrix products  246 us (35%)
  Pallas kernels  216 us (31%)
  other arithmetic  74.9 us (11%)
  blocking collectives  55.7 us (8%)
  local copies, waits for them, and re-layouts  48.4 us (7%)
  waiting for transfers between devices  33.4 us (5%)
  between operations  17.9 us (3%)
    pallas_call x1, Pallas kernels, reduce_rows(): pl.pallas_call(functools.partial(reduce_kernel, outer), out_shape=(jax.Sh...  172 us
    pallas_call x4, Pallas kernels, adam_call(): pl.pallas_call(functools.partial(adam_kernel, rate), grid=grid, out_shape...  44.5 us
    psum x1, blocking collectives, on_device(): total_valid = lax.psum(jnp.sum(valid), 'rows')  42.7 us
    dot_general x1, matrix products, attend_back(): jnp.einsum('hqk,qhd->khd', grad_raw, queries, preferred_element_type=jnp....  35.5 us
    dot_general x1, matrix products, attend_back(): jnp.einsum('hqk,khd->qhd', grad_raw, keys_in, preferred_element_type=jnp....  35.2 us
    dot_general x2, matrix products, forward(): jnp.dot(activated, down_low, preferred_element_type=jnp.float32)  28.1 us
    unnamed x164, local copies, waits for them, and re-layouts  24 us
    dot_general x2, matrix products, attend_block(): jnp.einsum('hqk,khd->qhd', probs, values, preferred_element_type=jnp.floa...  22.4 us
  transfers between devices with their start and end apart: 12, of which 6 were waited for; matrix products, arithmetic and copies ran while one was open for 22% of the time, Pallas kernels for 31%

profile of v1, /device:TPU:0, one launch (start us, length us, event | category | flops | bytes accessed | tf_op | source)
XLA Modules:
  0.0 693.2 jit_solution(15324614236301793397)
XLA Ops:
  14.6 7.5 %all-gather.19.cloned.1.call-done = bf16[1,1024,768]{2,1,0:T(8,128)(2,1)} async-done(((bf16[1,1024,384]{2,1,0:T(8,128)(2,1)}), bf16[1,1024,768]{2,1,0:T(8,128)(2,1)}) %all-gather.19.cloned.1.call-update) | async-done | bytes 1572880 | tf_op jit(solution)/shard_map/all_gather | solution.py:30
  27.5 7.1 %all-gather.17.cloned.1.call-done = bf16[1,1024,768]{2,1,0:T(8,128)(2,1)} async-done(((bf16[1,1024,384]{2,1,0:T(8,128)(2,1)}), bf16[1,1024,768]{2,1,0:T(8,128)(2,1)}) %all-gather.17.cloned.1.call-update) | async-done | bytes 1572880 | tf_op jit(solution)/shard_map/all_gather | solution.py:30
  40.6 15.3 %fusion.154 = (f32[6,1024]{1,0:T(8,128)S(1)}, f32[6,1024,1024]{1,2,0:T(8,128)}) fusion(pred[1024,1024]{0,1:T(8,128)(4,1)S(1)} %compare_and_fusion, bf16[1024,6,64]{0,2,1:T(8,128)(2,1)} %bitcast.141, bf16[1024,6,64]{0,2,1:T(8,128)(2,1)} %bitcast.140), kind=kOutput, calls=%fused_computation.249 | convolution fusion | flops 830473216 | bytes 27811840 | tf_op jit(solution)/shard_map/while/body/eval_jaxpr/sub | solution.py:76
  55.9 10.8 %fusion.71 = bf16[6,64,1024]{2,1,0:T(8,128)(2,1)S(1)} fusion(bf16[1024,6,64]{0,2,1:T(8,128)(2,1)} %bitcast.139, f32[6,1024,1024]{1,2,0:T(8,128)} %get-tuple-element.249, f32[6,1024]{1,0:T(8,128)S(1)} %get-tuple-element.248), kind=kOutput, calls=%fused_computation.122 | convolution fusion | flops 818282496 | bytes 26763264 | tf_op jit(solution)/shard_map/while/body/eval_jaxpr/hqk,khd->qhd/dot_general | solution.py:79
  69.4 13.0 %fusion.5 = (f32[6,1024]{1,0:T(8,128)S(1)}, f32[6,1024,1024]{1,2,0:T(8,128)}) fusion(pred[1024,1024]{0,1:T(8,128)(4,1)S(1)} %compare_and_fusion, bf16[1024,6,64]{0,2,1:T(8,128)(2,1)} %bitcast.133, bf16[1024,6,64]{0,2,1:T(8,128)(2,1)} %bitcast.135), kind=kOutput, calls=%fused_computation.14 | convolution fusion | flops 824174592 | bytes 27811840 | tf_op jit(solution)/shard_map/while/body/eval_jaxpr/qhd,khd->hqk/dot_general | solution.py:67
  82.4 11.3 %fusion.3 = f32[6,1024]{1,0:T(8,128)S(1)} fusion(f32[6,1024,1024]{1,2,0:T(8,128)} %get-tuple-element.247, f32[6,1024]{1,0:T(8,128)S(1)} %get-tuple-element.246, pred[1024,1024]{0,1:T(8,128)(4,1)S(1)} %compare_and_fusion), kind=kLoop, calls=%fused_computation.12 | loop fusion | flops 25159680 | bytes 26263552 | tf_op jit(solution)/shard_map/while/body/eval_jaxpr/reduce_sum | solution.py:77
  94.4 11.7 %fusion.38 = f32[6,64,1024]{2,1,0:T(8,128)S(1)} fusion(bf16[1024,6,64]{0,2,1:T(8,128)(2,1)S(1)} %bitcast.137, f32[6,1024,1024]{1,2,0:T(8,128)} %get-tuple-element.247, f32[6,1024]{1,0:T(8,128)S(1)} %fusion.3, f32[6,1024]{1,0:T(8,128)S(1)} %get-tuple-element.246, pred[1024,1024]{0,1:T(8,128)(4,1)S(1)} %compare_and_fusion), kind=kOutput, calls=%fused_computation.32 | convolution fusion | flops 836763648 | bytes 28622848 | tf_op jit(solution)/shard_map/while/body/eval_jaxpr/hqk,khd->qhd/dot_general | solution.py:79
  117.1 5.4 reduce-scatter.11.cloned.1.call-done
  145.2 21.5 %fusion.57 = f32[1024,768]{1,0:T(8,128)} fusion(bf16[1536,768]{1,0:T(8,128)(2,1)S(1)} %copy-done, bf16[1024,768]{1,0:T(8,128)(2,1)} %all-gather.11.cloned.1.call-done, bf16[768,1536]{1,0:T(8,128)(2,1)} %param.67, f32[1536]{0:T(1024)} %convert_element_type.147), kind=kOutput, calls=%fused_computation.84 | convolution fusion | flops 4935647232 | bytes 9443328 | tf_op jit(solution)/shard_map/dot_general | solution.py:128
  167.4 20.2 %multiply_convert_fusion.1 = (bf16[1024,1536]{1,0:T(8,128)(2,1)S(1)}, f32[1024,1536]{1,0:T(8,128)}, f32[1024,1536]{1,0:T(8,128)}) fusion(f32[1536]{0:T(1024)S(1)} %copy-done.72, f32[1536]{0:T(1024)S(1)} %copy-done.60, bf16[1024,768]{1,0:T(8,128)(2,1)} %all-gather.9.cloned.1.call-done, f32[768,1536]{1,0:T(8,128)} %weight_ref.6), kind=kOutput, calls=%fused_computation.55 | convolution fusion | flops 2522480640 | bytes 22032384 | tf_op jit(solution)/shard_map/dot_general | solution.py:126
  189.2 6.6 fusion.75
  197.2 42.7 %psum.95 = f32[]{:T(128)} all-reduce(f32[]{:T(128)} %convert_reduce_fusion.2), channel_id=1, replica_groups=mesh['rows'=16,'hid'=2] {'rows'}, use_global_device_ids=true, to_apply=%region_13.14 | all-reduce | flops 1 | bytes 8 | tf_op jit(solution)/shard_map/psum | solution.py:528
  263.7 6.0 all-gather.13.cloned.1.call-done
  269.7 11.8 %convert_reduce_fusion = (f32[1536]{0:T(1024)}, bf16[1024,1536]{1,0:T(8,128)(2,1)S(1)}) fusion(f32[1024,1536]{1,0:T(8,128)} %get-tuple-element.200, f32[1536]{0:T(1024)S(1)} %copy-done.72, bf16[1024,768]{1,0:T(8,128)(2,1)} %all-gather.13.cloned.1.call-done, f32[1536,768]{1,0:T(8,128)} %weight_ref.7, f32[1024,1536]{1,0:T(8,128)} %get-tuple-element.250, ...), kind=kOutput, calls=%fused_computation.40 | convolution fusion | flops 2448554496 | bytes 22038528 | tf_op jit(solution)/shard_map/dot_general | solution.py:539
  283.2 6.1 convolution_convert_fusion.3
  332.0 10.1 %fusion.138 = f32[6,1024,1024]{1,2,0:T(8,128)} fusion(bf16[1024,6,64]{0,2,1:T(8,128)(2,1)S(1)} %bitcast.138, f32[1024,6,64]{0,2,1:T(8,128)S(1)} %bitcast.129, f32[6]{0:T(128)S(1)} %copy-done.48), kind=kOutput, calls=%fused_computation.237 | convolution fusion | flops 806092800 | bytes 27525144 | tf_op jit(solution)/shard_map/while/body/eval_jaxpr/qhd,khd->hqk/dot_general | solution.py:87
  342.1 12.5 %fusion.62 = bf16[6,64,1024]{2,1,0:T(8,128)(2,1)} fusion(f32[6,1024,1024]{1,2,0:T(8,128)} %get-tuple-element.247, f32[6,1024]{1,0:T(8,128)S(1)} %copy-done.44, pred[1024,1024]{0,1:T(8,128)(4,1)S(1)} %copy-done.10, f32[1024,6,64]{0,2,1:T(8,128)S(1)} %bitcast.130, f32[6]{0:T(128)S(1)} %copy-done.48), kind=kOutput, calls=%fused_computation.119 | convolution fusion | flops 831651840 | bytes 28598296 | tf_op jit(solution)/shard_map/while/body/eval_jaxpr/hqk,qhd->khd/dot_general | solution.py:94
  354.6 35.2 %fusion.65 = bf16[6,64,1024]{2,1,0:T(8,128)(2,1)} fusion(bf16[1024,6,64]{0,2,1:T(8,128)(2,1)} %bitcast.136, f32[6,1024,1024]{1,2,0:T(8,128)} %fusion.138, f32[6,1024,1024]{1,2,0:T(8,128)} %get-tuple-element.247, f32[6,1024]{1,0:T(8,128)S(1)} %copy-done.44, pred[1024,1024]{0,1:T(8,128)(4,1)S(1)} %copy-done.10), kind=kOutput, calls=%fused_computation.120 | convolution fusion | flops 874912768 | bytes 52977664 | tf_op jit(solution)/shard_map/while/body/eval_jaxpr/hqk,khd->qhd/dot_general | solution.py:92
  389.8 35.5 %fusion.68 = bf16[6,64,1024]{2,1,0:T(8,128)(2,1)} fusion(bf16[1024,6,64]{0,2,1:T(8,128)(2,1)S(1)} %bitcast.134, f32[6,1024,1024]{1,2,0:T(8,128)} %fusion.138, f32[6,1024,1024]{1,2,0:T(8,128)} %get-tuple-element.247, f32[6,1024]{1,0:T(8,128)S(1)} %copy-done.44, pred[1024,1024]{0,1:T(8,128)(4,1)S(1)} %copy-done.10), kind=kOutput, calls=%fused_computation.121 | convolution fusion | flops 874912768 | bytes 52977664 | tf_op jit(solution)/shard_map/while/body/eval_jaxpr/hqk,qhd->khd/dot_general | solution.py:93
  431.0 5.8 bitcast_convert_fusion
  456.4 171.8 %reduce_rows.1 = (bf16[3,2,1536,384]{3,2,1,0:T(8,128)(2,1)}, f32[40,128]{1,0:T(8,128)}, f32[8,128]{1,0:T(8,128)}) custom-call(bf16[3,2,1536,384]{3,2,1,0:T(8,128)(2,1)} %pad_maximum_fusion.parts_ref, f32[40,128]{1,0:T(8,128)} %maximum_bitcast_fusion.7.small_ref), custom_call_target="tpu_custom_call" | custom-call | flops 100000000 | bytes 300000000 | tf_op jit(solution)/shard_map/reduce_rows/pallas_call | solution.py:349
  637.8 11.3 %adam.4 = (f32[3,768,384]{2,1,0:T(8,128)}, f32[3,768,384]{2,1,0:T(8,128)}, f32[3,768,384]{2,1,0:T(8,128)}, bf16[3,768,384]{2,1,0:T(8,128)(2,1)}) custom-call(f32[8,128]{1,0:T(8,128)S(1)} %copy-done.7, bf16[3,2,1536,384]{3,2,1,0:T(8,128)(2,1)} %get-tuple-element.126.sums_ref, f32[3,768,384]{2,1,0:T(8,128)S(1)} %copy-done.3, f32[3,768,384]{2,1,0:T(8,128)} %first_ref.4, ...), custom_call_target="tpu_custom_call" | custom-call | flops 17694720 | bytes 24772608 | tf_op jit(solution)/shard_map/adam/pallas_call | solution.py:418
  649.1 14.5 %adam.7 = (f32[1536,768]{1,0:T(8,128)}, f32[1536,768]{1,0:T(8,128)}, f32[1536,768]{1,0:T(8,128)}, bf16[1536,768]{1,0:T(8,128)(2,1)}) custom-call(f32[8,128]{1,0:T(8,128)S(1)} %copy-done.7, bf16[3,2,1536,384]{3,2,1,0:T(8,128)(2,1)} %get-tuple-element.126.sums_ref, f32[1536,768]{1,0:T(8,128)S(1)} %bitcast.126, f32[1536,768]{1,0:T(8,128)} %first_ref.7, ...), custom_call_target="tpu_custom_call" | custom-call | flops 23592960 | bytes 33030144 | tf_op jit(solution)/shard_map/adam/pallas_call | solution.py:418
  663.8 14.4 %adam.6 = (f32[768,1536]{1,0:T(8,128)}, f32[768,1536]{1,0:T(8,128)}, f32[768,1536]{1,0:T(8,128)}, bf16[768,1536]{1,0:T(8,128)(2,1)}) custom-call(f32[8,128]{1,0:T(8,128)S(1)} %copy-done.7, bf16[3,2,1536,384]{3,2,1,0:T(8,128)(2,1)} %get-tuple-element.126.sums_ref, f32[768,1536]{1,0:T(8,128)S(1)} %bitcast.128, f32[768,1536]{1,0:T(8,128)} %first_ref.6, ...), custom_call_target="tpu_custom_call" | custom-call | flops 23592960 | bytes 33030144 | tf_op jit(solution)/shard_map/adam/pallas_call | solution.py:418
  (290 shorter events, 167.2 us)
Async XLA Ops:
  7.2 138.0 %copy-start = (bf16[1536,768]{1,0:T(8,128)(2,1)S(1)}, bf16[1536,768]{1,0:T(8,128)(2,1)}, u32[]{:S(2)}) copy-start(bf16[1536,768]{1,0:T(8,128)(2,1)} %param.68) | copy-start | bytes 7077892
  7.2 14.9 %all-gather.19.cloned.1.call-start = ((), (), s32[]{:S(2)}) async-start(), calls=%async_computation.15 | async-start | bytes 2359296 | tf_op jit(solution)/shard_map/all_gather | solution.py:30
  8.0 26.6 %all-gather.17.cloned.1.call-start = ((), (), s32[]{:S(2)}) async-start(), calls=%async_computation.14 | async-start | bytes 2359296 | tf_op jit(solution)/shard_map/all_gather | solution.py:30
  8.7 104.9 %reduce-scatter.15.cloned.1.call-start = ((), (), s32[]{:S(2)}) async-start(), calls=%async_computation.9 | async-start | bytes 4718592 | tf_op jit(solution)/shard_map/reduce_scatter | solution.py:34
  11.8 110.8 %copy-start.46 = (f32[384]{0:T(512)}, f32[384]{0:T(512)S(1)}, u32[]{:S(2)}) copy-start(f32[384]{0:T(512)S(1)} %get-tuple-element.224) | copy-start | bytes 4612
  11.8 125.6 %copy-start.37 = (f32[384]{0:T(512)}, f32[384]{0:T(512)S(1)}, u32[]{:S(2)}) copy-start(f32[384]{0:T(512)S(1)} %get-tuple-element.225) | copy-start | bytes 4612
  14.6 79.2 %copy-start.9 = (pred[1024,1024]{0,1:T(8,128)(4,1)}, pred[1024,1024]{0,1:T(8,128)(4,1)S(1)}, u32[]{:S(2)}) copy-start(pred[1024,1024]{0,1:T(8,128)(4,1)S(1)} %compare_and_fusion) | copy-start | bytes 3145732
  69.4 53.2 %reduce-scatter.11.cloned.1.call-start = ((), (), s32[]{:S(2)}) async-start(), calls=%async_computation.6 | async-start | bytes 4718592 | tf_op jit(solution)/shard_map/reduce_scatter | solution.py:34
  110.4 34.8 %all-gather.11.cloned.1.call-start = ((), (), s32[]{:S(2)}) async-start(), calls=%async_computation.10 | async-start | bytes 2359296 | tf_op jit(solution)/shard_map/all_gather | solution.py:30
  134.0 32.8 %all-gather.9.cloned.1.call-start = ((), (), s32[]{:S(2)}) async-start(), calls=%async_computation.7 | async-start | bytes 2359296 | tf_op jit(solution)/shard_map/all_gather | solution.py:30
  142.2 100.3 %reduce-scatter.17.cloned.1.call-start = ((), (), s32[]{:S(2)}) async-start(), calls=%async_computation.11 | async-start | bytes 4718592 | tf_op jit(solution)/shard_map/reduce_scatter | solution.py:34
  166.7 78.8 %reduce-scatter.13.cloned.1.call-start = ((), (), s32[]{:S(2)}) async-start(), calls=%async_computation.8 | async-start | bytes 4718592 | tf_op jit(solution)/shard_map/reduce_scatter | solution.py:34
  195.9 46.6 %copy-start.42 = (f32[384]{0:T(512)S(1)}, f32[384]{0:T(512)}, u32[]{:S(2)}) copy-start(f32[384]{0:T(512)} %copy-done.41) | copy-start | bytes 4612
  195.9 46.6 %copy-start.43 = (f32[384]{0:T(512)S(1)}, f32[384]{0:T(512)}, u32[]{:S(2)}) copy-start(f32[384]{0:T(512)} %get-tuple-element.162) | copy-start | bytes 4612
  195.9 46.6 %copy-start.54 = (f32[384]{0:T(512)S(1)}, f32[384]{0:T(512)}, u32[]{:S(2)}) copy-start(f32[384]{0:T(512)} %get-tuple-element.161) | copy-start | bytes 4612
  195.9 49.6 %copy-start.38 = (f32[384]{0:T(512)S(1)}, f32[384]{0:T(512)}, u32[]{:S(2)}) copy-start(f32[384]{0:T(512)} %copy-done.37) | copy-start | bytes 4612
  195.9 49.6 %copy-start.53 = (f32[384]{0:T(512)S(1)}, f32[384]{0:T(512)}, u32[]{:S(2)}) copy-start(f32[384]{0:T(512)} %get-tuple-element.226) | copy-start | bytes 4612
  195.9 73.8 %all-gather.13.cloned.1.call-start = ((), (), s32[]{:S(2)}) async-start(), calls=%async_computation.12 | async-start | bytes 2359296 | tf_op jit(solution)/shard_map/all_gather | solution.py:38
  263.7 43.1 %reduce-scatter.19.cloned.1.call-start = ((), (), s32[]{:S(2)}) async-start(), calls=%async_computation.16 | async-start | bytes 2359296
  292.0 37.7 %all-gather.15.cloned.1.call-start = ((), (), s32[]{:S(2)}) async-start(), calls=%async_computation.13 | async-start | bytes 2359296 | tf_op jit(solution)/shard_map/all_gather | solution.py:38
  318.6 362.2 %reduce-scatter.21.cloned.1.call-start = ((), (), s32[]{:S(2)}) async-start(), calls=%async_computation.17 | async-start | bytes 2359296
  456.4 176.4 %copy-start.4 = (f32[384,768]{1,0:T(8,128)S(1)}, f32[384,768]{1,0:T(8,128)}, u32[]{:S(2)}) copy-start(f32[384,768]{1,0:T(8,128)} %first_ref.5) | copy-start | bytes 3538948
  456.4 176.4 %copy-start.5 = (f32[384,768]{1,0:T(8,128)S(1)}, f32[384,768]{1,0:T(8,128)}, u32[]{:S(2)}) copy-start(f32[384,768]{1,0:T(8,128)} %second_ref.5) | copy-start | bytes 3538948
  632.8 47.4 %copy-start.33 = (f32[6,384]{1,0:T(8,128)}, f32[6,384]{1,0:T(8,128)S(1)}, u32[]{:S(2)}) copy-start(f32[6,384]{1,0:T(8,128)S(1)} %reshape.227) | copy-start | bytes 27652
  (68 other events, 616.5 us)
Sparse Core Ops, SparseCore 0:
  9.6 12.4 all-gather.18
  23.6 10.9 all-gather.16
  69.5 12.0 reduce-scatter.14
  110.5 12.0 reduce-scatter.10
  134.1 11.0 all-gather.10
  147.1 10.9 all-gather.8
  166.8 12.0 reduce-scatter.16
  196.0 12.0 reduce-scatter.12
  263.8 5.8 all-gather.12
  292.1 10.1 reduce-scatter.18
  318.7 10.9 all-gather.14
  443.9 10.2 reduce-scatter.20
